TPU v7x, 32 devices: a whole 2x2x4 slice. The times are simulated.
32 devices in a mesh: lon: 8 (over z, core), lat: 4 (over y, x).
Axes of the slice: x: 2, y: 2, z: 4, core: 2. Of those that a mesh axis runs over, the one named last changes fastest.
Arguments:
- adjoint_height: float32 [2048, 1024], P('lat', 'lon'), may hold values from -6 to 6
- depth: float32 [2048, 1024], P('lat', 'lon'), may hold values from 0.1 to 1
- wet: int32 [2048, 1024], P('lat', 'lon'), may hold values 0 or 1
- basis_lat: float32 [32, 2048], P(None, 'lat'), may hold values from -1.5 to 1.5
- basis_lon: float32 [32, 1024], P(None, 'lon'), may hold values from -1.5 to 1.5
- tile_owner: int32 [128, 64], P('lat', 'lon'), may hold values from 0 to 7, as said below
- tile_patch: int32 [128, 64], P('lat', 'lon'), may hold values from 0 to 255
- tile_count: int32 [128, 64], P('lat', 'lon'), may hold values from 1 to 32
- prior_patches: float32 [4, 8, 256, 256], P('lat', 'lon'), may hold values from 0 to 11
- prior_subfaults: float32 [32, 32], replicated, may hold values from -0.4 to 1.7
Outputs:
- adjoint_final: float32 [2048, 1024], P('lat', 'lon')
- source_gradient: float32 [2048, 1024], P('lat', 'lon')
Inputs may be any that keep to these rules, and one draw needn't show every extreme that they name: `tile_owner`: within each device's block of tiles no owner is named more than 56 times, and in every latitude band one owner is named exactly 56 times by every device's block.
All inputs are finite; a program needn't handle non-finite values. No bound on the sum of `wet` on one device may be relied on, other than what follows from the above.
Results may differ from a plain program's by a relative error of at most 0.0002.
Values sent between devices are 32-bit elements; how exact they have to be, the bound alone decides.
A program may use at most 64 MiB of HBM per device.

v0:
```python
import functools

import jax
import jax.numpy as jnp
from jax import lax
from jax.experimental import pallas as pl
from jax.experimental.pallas import tpu as pltpu
from jax.sharding import PartitionSpec as P

STEPS = 4
PARTS = 2
TS = 16
SUB = 32
NPATCH = 256
COURANT = 0.6
GROUPS = 4
CHUNK = 128
MESH = pl.DeviceIdType.MESH

F32 = jnp.float32
BF16 = jnp.bfloat16


def iota(shape, dim):
    return lax.broadcasted_iota(jnp.int32, shape, dim)


def div(x, n):
    return lax.shift_right_logical(x, n.bit_length() - 1) if n & (n - 1) == 0 else x // n


def mod(x, n):
    return x & (n - 1) if n & (n - 1) == 0 else x % n


def lanes(n):
    return iota((1, n), 1)


def rows_of(n):
    return iota((n, 1), 0)


def hot(mask):
    return jnp.where(mask, 1.0, 0.0).astype(BF16)


def split(x):
    high = x.astype(BF16)
    return high, (x - high.astype(F32)).astype(BF16)


def dot(a, b, contract=((1,), (0,))):
    return lax.dot_general(a, b, (contract, ((), ())), preferred_element_type=F32)


def select_dot(mask, x):
    width = x.shape[1]
    high, low = split(x)
    both = dot(mask, jnp.concatenate([high, low], axis=1))
    return both[:, :width] + both[:, width:]


def terms(x):
    high, rest = x.astype(BF16), x
    rest = x - high.astype(F32)
    middle = rest.astype(BF16)
    return high, middle, (rest - middle.astype(F32)).astype(BF16)


def kernel(
    lon_count,
    lat_count,
    slot_rows,
    height_hbm,
    depth_hbm,
    wet_hbm,
    basis_lat_hbm,
    basis_lon_hbm,
    owner_hbm,
    patch_hbm,
    count_hbm,
    prior_patches_hbm,
    prior_subfaults_hbm,
    height_out,
    gradient,
    lat_wide,
    lon_high,
    lon_low,
    height_in,
    depth_in,
    wet_in,
    basis_lat,
    basis_lon,
    owner_in,
    patch_in,
    count_in,
    prior_patches,
    prior_subfaults,
    edge_send,
    edge_recv,
    side_send,
    side_recv,
    height_ext,
    depth_ext,
    patch_send,
    patch_recv,
    value_send,
    value_recv,
    reply_send,
    reply_recv,
    place,
    place_back,
    member,
    member_prior,
    mixing,
    active,
    input_sem,
    halo_send_sem,
    halo_recv_sem,
    peer_send_sem,
    peer_recv_sem,
):
    loads = [
        pltpu.make_async_copy(src, dst, input_sem.at[index])
        for index, (src, dst) in enumerate(
            (
                (height_hbm, height_in),
                (depth_hbm, depth_in),
                (wet_hbm, wet_in),
                (owner_hbm, owner_in),
                (patch_hbm, patch_in),
                (count_hbm, count_in),
                (basis_lat_hbm, basis_lat),
                (basis_lon_hbm, basis_lon),
                (prior_subfaults_hbm, prior_subfaults),
                (prior_patches_hbm, prior_patches),
            )
        )
    ]
    for load in loads:
        load.start()
    lat = lax.axis_index("lat")
    lon = lax.axis_index("lon")
    rows, cols = height_in.shape
    tile_rows, tile_cols = rows // TS, cols // TS
    tiles = tile_rows * tile_cols
    block = lon_count * slot_rows
    slots = GROUPS * block
    up, down = lax.rem(lat + lat_count - 1, lat_count), lax.rem(lat + 1, lat_count)
    left, right = lax.rem(lon + lon_count - 1, lon_count), lax.rem(lon + 1, lon_count)

    def peer(offset):
        return lax.rem(lon + offset, lon_count)

    def each_peer(body):
        if lon_count <= 8:
            for offset in range(1, lon_count):
                body(offset)
        else:
            def step(offset, carry):
                body(offset)
                return carry

            lax.fori_loop(1, lon_count, step, 0)

    barrier = pltpu.get_barrier_semaphore()

    def greet(lat_at, lon_at):
        pl.semaphore_signal(barrier, inc=1, device_id=(lon_at, lat_at), device_id_type=MESH)

    each_peer(lambda offset: greet(lat, peer(offset)))
    for lat_at in (up, down):
        for lon_at in (left, lon, right):
            greet(lat_at, lon_at)

    for load in loads[:3]:
        load.wait()
    wet_depth = depth_in[...] * wet_in[...].astype(F32)
    edge_send[0:8, :] = height_in[0:8, :]
    edge_send[8:16, :] = wet_depth[0:8, :]
    edge_send[16:24, :] = height_in[rows - 8 : rows, :]
    edge_send[24:32, :] = wet_depth[rows - 8 : rows, :]
    fields = jnp.concatenate([height_in[...], wet_depth], axis=1)

    def rim_mask():
        row, lane = rows_of(16), lanes(2 * cols)
        wanted = jnp.where(row < 8, row & 3, cols - 4 + (row & 3))
        return hot(mod(lane, cols) == wanted) * hot(div(lane, cols) == (div(row, 4) & 1))

    rim = rim_mask()
    side_send[...] = sum(dot(rim, term, ((1,), (1,))) for term in terms(fields))

    pl.semaphore_wait(barrier, lon_count - 1 + 6)

    halo = []

    def send_halo(src, dst, lat_at, lon_at):
        index = len(halo)
        copy = pltpu.make_async_remote_copy(
            src_ref=src,
            dst_ref=dst,
            send_sem=halo_send_sem.at[index],
            recv_sem=halo_recv_sem.at[index],
            device_id=(lon_at, lat_at),
            device_id_type=MESH,
        )
        copy.start()
        halo.append(copy)

    send_halo(side_send.at[pl.ds(0, 8)], side_recv.at[pl.ds(0, 8)], lat, left)
    send_halo(side_send.at[pl.ds(8, 8)], side_recv.at[pl.ds(8, 8)], lat, right)
    for place_at, lon_at in ((0, lon), (1, left), (2, right)):
        send_halo(edge_send.at[pl.ds(0, 16)], edge_recv.at[place_at], up, lon_at)
    for place_at, lon_at in ((3, lon), (4, left), (5, right)):
        send_halo(edge_send.at[pl.ds(16, 16)], edge_recv.at[place_at], down, lon_at)

    for load in loads[3:]:
        load.wait()
    wide = tile_cols * SUB
    wide_line = lanes(wide)
    repeat_sub = hot(mod(wide_line, SUB) == rows_of(SUB))
    stacked = jnp.concatenate([repeat_sub] * 3, axis=0)
    lat_wide[...] = dot(
        jnp.concatenate(terms(basis_lat[...]), axis=0), stacked, ((0,), (0,))
    )
    lon_wide = dot(jnp.concatenate(terms(basis_lon[...]), axis=0), stacked, ((0,), (0,)))
    lon_wide = jnp.where(div(rows_of(cols), TS) == div(wide_line, SUB), lon_wide, 0.0)
    lon_high[...], lon_low[...] = split(lon_wide)
    count_wide = dot(
        count_in[...].astype(F32).astype(BF16),
        hot(div(wide_line, SUB) == rows_of(tile_cols)),
        ((0,), (0,)),
    )
    active[...] = jnp.where(mod(wide_line, SUB).astype(F32) < count_wide, 1.0, 0.0)
    repeat_groups = hot(mod(lanes(128), SUB) == rows_of(SUB))
    across = jnp.concatenate([prior_subfaults[...]] * tile_cols, axis=0)
    across_high, across_low = split(across)
    mixing[:wide] = dot(across_high, repeat_groups).astype(BF16)
    mixing[wide:] = dot(across_low, repeat_groups).astype(BF16)

    tile_line, tile_stack = lanes(tiles), rows_of(tiles)

    def as_row(values):
        spread = dot(
            values.astype(F32).astype(BF16),
            hot(mod(tile_line, tile_rows) == rows_of(tile_rows)),
        )
        keep = div(tile_line, tile_rows) == rows_of(tile_cols)
        return jnp.sum(jnp.where(keep, spread, 0.0), axis=0, keepdims=True)

    owner_row = as_row(owner_in[...])
    owner_spread = dot(
        hot(div(tile_stack, tile_rows) == lanes(tile_cols)),
        owner_in[...].astype(F32).astype(BF16),
    )
    owner_column = jnp.sum(
        jnp.where(mod(tile_stack, tile_rows) == lanes(tile_rows), owner_spread, 0.0),
        axis=1,
        keepdims=True,
    )
    earlier = jnp.where((owner_column == owner_row) & (tile_stack < tile_line), 1.0, 0.0)
    rank_row = jnp.sum(earlier, axis=0, keepdims=True)

    def slot_of(owner, rank):
        owner, rank = owner.astype(jnp.int32), rank.astype(jnp.int32)
        return div(rank, slot_rows) * block + owner * slot_rows + mod(rank, slot_rows)

    place[...] = hot(rows_of(slots) == slot_of(owner_row, rank_row))
    patch_lines = jnp.broadcast_to(as_row(patch_in[...]), (128, tiles)).astype(BF16)
    sent_patch = dot(place[...], patch_lines, ((1,), (1,)))
    packed = jnp.zeros((block, 128), F32)
    for group in range(GROUPS):
        packed = jnp.where(
            lanes(128) == group, sent_patch[group * block : (group + 1) * block], packed
        )
    patch_send[...] = packed

    sent = []

    def exchange(send, recv, phase):
        def descriptor(offset):
            target = peer(offset)
            return pltpu.make_async_remote_copy(
                src_ref=send.at[pl.ds(pl.multiple_of(target * slot_rows, 8), slot_rows)],
                dst_ref=recv.at[pl.ds(pl.multiple_of(lon * slot_rows, 8), slot_rows)],
                send_sem=peer_send_sem.at[phase, offset],
                recv_sem=peer_recv_sem.at[phase, offset],
                device_id=(target, lat),
                device_id_type=MESH,
            )

        each_peer(lambda offset: descriptor(offset).start())
        own = pl.ds(pl.multiple_of(lon * slot_rows, 8), slot_rows)
        recv[own, :] = send[own, :]
        sent.append(lambda: each_peer(lambda offset: descriptor(offset).wait_send()))
        return lambda: each_peer(lambda offset: descriptor(offset).wait_recv())

    patches_done = exchange(patch_send, patch_recv, 0)

    height_ext[4 : rows + 4, :cols] = height_in[...]
    depth_ext[4 : rows + 4, :cols] = wet_depth
    for copy in halo:
        copy.wait_recv()

    side_terms = jnp.concatenate(terms(side_recv[...]), axis=0)
    sides = dot(side_terms, jnp.concatenate([rim_mask()] * 3, axis=0), ((0,), (0,)))
    edge_lane = iota((8, cols), 1)
    for at, ext in ((0, height_ext), (8, depth_ext)):
        ext[4 : rows + 4, cols:] = sides[:, :cols] if at == 0 else sides[:, cols:]
        below = jnp.concatenate(
            [
                edge_recv[0, at : at + 8, :],
                jnp.where(edge_lane < cols // 2, edge_recv[1, at : at + 8, :], edge_recv[2, at : at + 8, :]),
            ],
            axis=1,
        )
        above = jnp.concatenate(
            [
                edge_recv[3, at : at + 8, :],
                jnp.where(edge_lane < cols // 2, edge_recv[4, at : at + 8, :], edge_recv[5, at : at + 8, :]),
            ],
            axis=1,
        )
        ext[0:4, :] = jnp.where(lat == 0, 0.0, above)[4:8]
        ext[rows + 4 : rows + 8, :] = jnp.where(lat == lat_count - 1, 0.0, below)[0:4]

    size = CHUNK + 8

    def stencil(chunk, carry):
        base = pl.ds(pl.multiple_of(chunk * CHUNK, 8), size)
        height, depth = height_ext[base, :], depth_ext[base, :]
        width = 2 * cols
        east_weight = COURANT * COURANT * jnp.minimum(depth, pltpu.roll(depth, width - 1, 1))
        north_weight = COURANT * COURANT * jnp.minimum(depth, pltpu.roll(depth, size - 1, 0))
        east = north = None
        for repeat in range(STEPS):
            east_add = east_weight * (pltpu.roll(height, width - 1, 1) - height)
            north_add = north_weight * (pltpu.roll(height, size - 1, 0) - height)
            east = east_add if repeat == 0 else east + east_add
            north = north_add if repeat == 0 else north + north_add
            height = (
                height
                + (east - pltpu.roll(east, 1, 1))
                + (north - pltpu.roll(north, 1, 0))
            )
        done = pltpu.roll(height[:, :cols], size - 4, 0)
        height_out[pl.ds(pl.multiple_of(chunk * CHUNK, 8), CHUNK), :] = done[:CHUNK]
        return carry

    lax.fori_loop(0, rows // CHUNK, stencil, 0)

    height_high, height_low = split(height_out[...])
    projected = dot(
        jnp.concatenate([height_high, height_low], axis=1),
        jnp.concatenate([lon_high[...], lon_high[...]], axis=0),
    ) + dot(height_high, lon_low[...])
    sensitivity = (
        jnp.sum((projected * lat_wide[...]).reshape(tile_rows, TS, wide), axis=1) * active[...]
    )
    alone = jnp.concatenate(
        [jnp.where(div(wide_line, SUB) == c, sensitivity, 0.0) for c in range(tile_cols)], axis=0
    )
    alone_high, alone_low = split(alone)
    by_tile = (
        dot(alone_high, mixing[:wide])
        + dot(alone_low, mixing[:wide])
        + dot(alone_high, mixing[wide:])
    )
    group_line = div(lanes(128), SUB)

    def pack(x):
        height = x.shape[0] // GROUPS
        packed = x[:height]
        for group in range(1, GROUPS):
            packed = jnp.where(group_line == group, x[group * height : (group + 1) * height], packed)
        return packed

    def unpack(x):
        return jnp.concatenate(
            [jnp.where(group_line == group, x, 0.0) for group in range(GROUPS)], axis=0
        )

    def over_groups(x):
        x = x + pltpu.roll(x, 2 * SUB, 1)
        return x + pltpu.roll(x, SUB, 1)

    value_send[...] = pack(select_dot(place[...], by_tile))
    values_done = exchange(value_send, value_recv, 1)

    patches_done()
    patch_ids = patch_recv[...]
    patch_line = patch_ids.T
    prior_terms = jnp.concatenate(split(prior_patches[...]), axis=1)
    for group in range(GROUPS):
        at = pl.ds(group * block, block)
        member[:, at] = hot(rows_of(NPATCH).astype(F32) == patch_line[group : group + 1, :])
        hit = hot(lanes(NPATCH).astype(F32) == patch_ids[:, group : group + 1])
        member_prior[at, :] = dot(hit, prior_terms).astype(BF16)

    values_done()
    par_high, par_low = split(over_groups(select_dot(member[...], unpack(value_recv[...]))))
    both = dot(
        member_prior[...],
        jnp.concatenate(
            [
                jnp.concatenate([par_high, par_low], axis=1),
                jnp.concatenate([par_high, jnp.zeros_like(par_low)], axis=1),
            ],
            axis=0,
        ),
    )
    reply_send[...] = pack(both[:, :128] + both[:, 128:])
    replies_done = exchange(reply_send, reply_recv, 2)
    later = jnp.where((owner_column == owner_row) & (tile_line < tile_stack), 1.0, 0.0)
    rank_column = jnp.sum(later, axis=1, keepdims=True)
    place_back[...] = hot(lanes(slots) == slot_of(owner_column, rank_column))
    replies_done()

    tile_value = over_groups(select_dot(place_back[...], unpack(reply_recv[...])))
    pieces = []
    for first in range(0, tile_cols, GROUPS):
        pieces.append(pack(tile_value[first * tile_rows : (first + GROUPS) * tile_rows]))
    tile_value = jnp.concatenate(pieces, axis=1) * active[...]
    part = rows // PARTS
    contract = ((1,), (1,))
    for index in range(PARTS):
        at = pl.ds(index * part, part)
        value = tile_value[index * part // TS : (index + 1) * part // TS, :]
        spread = jnp.broadcast_to(value[:, None, :], (part // TS, TS, wide)).reshape(part, wide)
        high, low = split(spread * lat_wide[at, :])
        gradient[at, :] = (
            dot(high, lon_high[...], contract)
            + dot(low, lon_high[...], contract)
            + dot(high, lon_low[...], contract)
        )
    for copy in halo:
        copy.wait_send()
    for wait in sent:
        wait()


def local(
    lon_count,
    lat_count,
    adjoint_height,
    depth,
    wet,
    basis_lat,
    basis_lon,
    tile_owner,
    tile_patch,
    tile_count,
    prior_patches,
    prior_subfaults,
):
    rows, cols = adjoint_height.shape
    tiles = (rows // TS) * (cols // TS)
    capacity = max(2, 7 * tiles // (4 * lon_count))
    slot_rows = 8 * pl.cdiv(capacity, 8 * GROUPS)
    block = lon_count * slot_rows
    slots = GROUPS * block
    wide = SUB * (cols // TS)
    hbm = pl.BlockSpec(memory_space=pltpu.HBM)
    packed = pltpu.VMEM((block, 128), F32)
    inputs = (
        adjoint_height,
        depth,
        wet,
        basis_lat,
        basis_lon,
        tile_owner.T,
        tile_patch.T,
        tile_count.T,
        prior_patches.reshape(NPATCH, NPATCH),
        prior_subfaults,
    )
    return pl.pallas_call(
        functools.partial(kernel, lon_count, lat_count, slot_rows),
        out_shape=(pltpu.VMEM((rows, cols), F32),) * 2,
        in_specs=[hbm] * 10,
        out_specs=(pl.BlockSpec(memory_space=pltpu.VMEM),) * 2,
        scratch_shapes=[
            pltpu.VMEM((rows, wide), F32),
            pltpu.VMEM((cols, wide), BF16),
            pltpu.VMEM((cols, wide), BF16),
            *(pltpu.VMEM(x.shape, x.dtype) for x in inputs),
            pltpu.VMEM((32, cols), F32),
            pltpu.VMEM((6, 16, cols), F32),
            pltpu.VMEM((16, rows), F32),
            pltpu.VMEM((16, rows), F32),
            pltpu.VMEM((rows + 8, 2 * cols), F32),
            pltpu.VMEM((rows + 8, 2 * cols), F32),
            packed,
            packed,
            packed,
            packed,
            packed,
            packed,
            pltpu.VMEM((slots, tiles), BF16),
            pltpu.VMEM((tiles, slots), BF16),
            pltpu.VMEM((NPATCH, slots), BF16),
            pltpu.VMEM((slots, 2 * NPATCH), BF16),
            pltpu.VMEM((2 * wide, 128), BF16),
            pltpu.VMEM((rows // TS, wide), F32),
            pltpu.SemaphoreType.DMA((10,)),
            pltpu.SemaphoreType.DMA((8,)),
            pltpu.SemaphoreType.DMA((8,)),
            pltpu.SemaphoreType.DMA((3, lon_count)),
            pltpu.SemaphoreType.DMA((3, lon_count)),
        ],
        compiler_params=pltpu.CompilerParams(
            collective_id=0, has_side_effects=True, vmem_limit_bytes=48 * 1024 * 1024
        ),
    )(*(pltpu.with_memory_space_constraint(x, pltpu.HBM) for x in inputs))


def solution(mesh):
    return jax.shard_map(
        functools.partial(local, mesh.shape["lon"], mesh.shape["lat"]),
        mesh=mesh,
        in_specs=(
            P("lat", "lon"),
            P("lat", "lon"),
            P("lat", "lon"),
            P(None, "lat"),
            P(None, "lon"),
            P("lat", "lon"),
            P("lat", "lon"),
            P("lat", "lon"),
            P("lat", "lon", None, None),
            P(),
        ),
        out_specs=(P("lat", "lon"), P("lat", "lon")),
        check_vma=False,
    )
```

profile of v0, /device:TPU:0, one launch (start us, length us, event | category | flops | bytes accessed | tf_op | source)
XLA Modules:
  0.0 26.3 jit_solution(3451795717875976464)
XLA Ops:
  0.6 24.2 %shard_map.113 = (f32[512,128]{1,0:T(8,128)S(1)}, f32[512,128]{1,0:T(8,128)S(1)}) custom-call(f32[512,128]{1,0:T(8,128)} %height_hbm.1, f32[512,128]{1,0:T(8,128)} %depth_hbm.1, s32[512,128]{1,0:T(8,128)} %wet_hbm.1, f32[32,512]{1,0:T(8,128)} %basis_lat_hbm.1, f32[32,128]{1,0:T(8,128)} %basis_lon_hbm.1, s32[8,32]{1,0:T(8,128)} %bitcast.5, s32[8,32]{1,0:T(8,128)} %bitcast.6, ...), custom_call_target="tpu_custom_call" | custom-call | tf_op jit(solution)/shard_map/pallas_call | solution.py:478
  24.9 0.7 %copy.14 = f32[512,128]{1,0:T(8,128)} copy(f32[512,128]{1,0:T(8,128)S(1)} %get-tuple-element.2) | data formatting | bytes 524288
  25.6 0.7 %copy.15 = f32[512,128]{1,0:T(8,128)} copy(f32[512,128]{1,0:T(8,128)S(1)} %get-tuple-element.3) | data formatting | bytes 524288
where the time goes:
time: 26.4 us; the launch traced here: 26.3 us
  Pallas kernels  24.2 us (92%)
  local copies, waits for them, and re-layouts  1.41 us (5%)
  between operations  0.64 us (2%)
    pallas_call x1, Pallas kernels, local(): pl.pallas_call(functools.partial(kernel, lon_count, lat_count, slot_rows)...  24.2 us
    unnamed x2, local copies, waits for them, and re-layouts  1.41 us

commit v1 on v0

--- a/solution.py
+++ b/solution.py
@@ -15,6 +15,7 @@
 COURANT = 0.6
 GROUPS = 4
 CHUNK = 128
+STRIP = 32
 MESH = pl.DeviceIdType.MESH
 
 F32 = jnp.float32
@@ -103,6 +104,8 @@
     side_recv,
     height_ext,
     depth_ext,
+    near_height,
+    near_depth,
     patch_send,
     patch_recv,
     value_send,
@@ -181,15 +184,36 @@
     edge_send[8:16, :] = wet_depth[0:8, :]
     edge_send[16:24, :] = height_in[rows - 8 : rows, :]
     edge_send[24:32, :] = wet_depth[rows - 8 : rows, :]
-    fields = jnp.concatenate([height_in[...], wet_depth], axis=1)
-
-    def rim_mask():
-        row, lane = rows_of(16), lanes(2 * cols)
-        wanted = jnp.where(row < 8, row & 3, cols - 4 + (row & 3))
-        return hot(mod(lane, cols) == wanted) * hot(div(lane, cols) == (div(row, 4) & 1))
-
-    rim = rim_mask()
-    side_send[...] = sum(dot(rim, term, ((1,), (1,))) for term in terms(fields))
+    line = lanes(cols)
+    strip = mod(line, STRIP)
+    groups = cols // STRIP
+    group_rows = rows // groups
+    sub_rows = group_rows // 4
+
+    def turn(x, by):
+        return x if by % cols == 0 else pltpu.roll(x, by % cols, 1)
+
+    def within(low, high):
+        return (strip >= low) & (strip < high)
+
+    def near_sides(field):
+        near = jnp.zeros((group_rows, cols), F32)
+        for g in range(groups):
+            part = field[g * group_rows : (g + 1) * group_rows]
+            here = div(line, STRIP) == g
+            near = jnp.where(here & within(4, 16), turn(part, g * STRIP + 4), near)
+            near = jnp.where(here & within(16, 28), turn(part, g * STRIP + 28 - cols), near)
+        return near
+
+    nears = [near_sides(height_in[...]), near_sides(wet_depth)]
+    for side, first in ((0, 4), (1, 24)):
+        message = jnp.zeros((sub_rows, cols), F32)
+        for k in range(4):
+            for field in range(2):
+                at = 8 * k + 4 * field
+                part = nears[field][k * sub_rows : (k + 1) * sub_rows]
+                message = jnp.where(within(at, at + 4), turn(part, at - first), message)
+        side_send[side] = message
 
     pl.semaphore_wait(barrier, lon_count - 1 + 6)
 
@@ -208,8 +232,8 @@
         copy.start()
         halo.append(copy)
 
-    send_halo(side_send.at[pl.ds(0, 8)], side_recv.at[pl.ds(0, 8)], lat, left)
-    send_halo(side_send.at[pl.ds(8, 8)], side_recv.at[pl.ds(8, 8)], lat, right)
+    send_halo(side_send.at[0], side_recv.at[0], lat, left)
+    send_halo(side_send.at[1], side_recv.at[1], lat, right)
     for place_at, lon_at in ((0, lon), (1, left), (2, right)):
         send_halo(edge_send.at[pl.ds(0, 16)], edge_recv.at[place_at], up, lon_at)
     for place_at, lon_at in ((3, lon), (4, left), (5, right)):
@@ -298,44 +322,13 @@
 
     patches_done = exchange(patch_send, patch_recv, 0)
 
-    height_ext[4 : rows + 4, :cols] = height_in[...]
-    depth_ext[4 : rows + 4, :cols] = wet_depth
-    for copy in halo:
-        copy.wait_recv()
-
-    side_terms = jnp.concatenate(terms(side_recv[...]), axis=0)
-    sides = dot(side_terms, jnp.concatenate([rim_mask()] * 3, axis=0), ((0,), (0,)))
-    edge_lane = iota((8, cols), 1)
-    for at, ext in ((0, height_ext), (8, depth_ext)):
-        ext[4 : rows + 4, cols:] = sides[:, :cols] if at == 0 else sides[:, cols:]
-        below = jnp.concatenate(
-            [
-                edge_recv[0, at : at + 8, :],
-                jnp.where(edge_lane < cols // 2, edge_recv[1, at : at + 8, :], edge_recv[2, at : at + 8, :]),
-            ],
-            axis=1,
-        )
-        above = jnp.concatenate(
-            [
-                edge_recv[3, at : at + 8, :],
-                jnp.where(edge_lane < cols // 2, edge_recv[4, at : at + 8, :], edge_recv[5, at : at + 8, :]),
-            ],
-            axis=1,
-        )
-        ext[0:4, :] = jnp.where(lat == 0, 0.0, above)[4:8]
-        ext[rows + 4 : rows + 8, :] = jnp.where(lat == lat_count - 1, 0.0, below)[0:4]
-
-    size = CHUNK + 8
-
-    def stencil(chunk, carry):
-        base = pl.ds(pl.multiple_of(chunk * CHUNK, 8), size)
-        height, depth = height_ext[base, :], depth_ext[base, :]
-        width = 2 * cols
-        east_weight = COURANT * COURANT * jnp.minimum(depth, pltpu.roll(depth, width - 1, 1))
+    def stencil(height, depth):
+        size = height.shape[0]
+        east_weight = COURANT * COURANT * jnp.minimum(depth, pltpu.roll(depth, cols - 1, 1))
         north_weight = COURANT * COURANT * jnp.minimum(depth, pltpu.roll(depth, size - 1, 0))
         east = north = None
         for repeat in range(STEPS):
-            east_add = east_weight * (pltpu.roll(height, width - 1, 1) - height)
+            east_add = east_weight * (pltpu.roll(height, cols - 1, 1) - height)
             north_add = north_weight * (pltpu.roll(height, size - 1, 0) - height)
             east = east_add if repeat == 0 else east + east_add
             north = north_add if repeat == 0 else north + north_add
@@ -344,11 +337,58 @@
                 + (east - pltpu.roll(east, 1, 1))
                 + (north - pltpu.roll(north, 1, 0))
             )
-        done = pltpu.roll(height[:, :cols], size - 4, 0)
-        height_out[pl.ds(pl.multiple_of(chunk * CHUNK, 8), CHUNK), :] = done[:CHUNK]
-        return carry
-
-    lax.fori_loop(0, rows // CHUNK, stencil, 0)
+        return pltpu.roll(height, size - 4, 0)[: size - 8]
+
+    height_ext[4 : rows + 4, :] = height_in[...]
+    depth_ext[4 : rows + 4, :] = wet_depth
+
+    def chunk(at):
+        base = slice(at, at + CHUNK + 8)
+        height_out[at : at + CHUNK, :] = stencil(height_ext[base, :], depth_ext[base, :])
+
+    for at in range(CHUNK, rows - CHUNK, CHUNK):
+        chunk(at)
+    for copy in halo:
+        copy.wait_recv()
+
+    for field, ext in ((0, height_ext), (1, depth_ext)):
+        at = slice(8 * field, 8 * field + 8)
+        below = [jnp.where(lat == lat_count - 1, 0.0, edge_recv[n, at, :]) for n in range(3)]
+        above = [jnp.where(lat == 0, 0.0, edge_recv[n, at, :]) for n in range(3, 6)]
+        ext[0:4, :] = above[0][4:8]
+        ext[rows + 4 : rows + 8, :] = below[0][0:4]
+        pieces = []
+        for k in range(4):
+            piece = nears[field][k * sub_rows : (k + 1) * sub_rows]
+            from_at = 8 * k + 4 * field
+            piece = jnp.where(within(0, 4), turn(side_recv[1], -from_at), piece)
+            pieces.append(jnp.where(within(28, 32), turn(side_recv[0], 28 - from_at), piece))
+
+        def corner(edges, inner, start):
+            middle, right_edge, left_edge = edges
+            outer = turn(left_edge, start + 4)
+            outer = jnp.where(within(4, 16), turn(middle, start + 4), outer)
+            outer = jnp.where(within(16, 28), turn(middle, start + 28), outer)
+            outer = jnp.where(within(28, 32), turn(right_edge, start + 28), outer)
+            return jnp.where(div(line, STRIP) == start // STRIP, outer, inner)
+
+        top = corner(above, turn(pieces[3][sub_rows - 8 :], STRIP), 0)
+        bottom = corner(below, turn(pieces[0][:8], -STRIP), cols - STRIP)
+        near = near_height if field == 0 else near_depth
+        near[0:4, :] = top[4:8]
+        for k in range(4):
+            near[4 + k * sub_rows : 4 + (k + 1) * sub_rows, :] = pieces[k]
+        near[group_rows + 4 : group_rows + 8, :] = bottom[0:4]
+
+    near_done = stencil(near_height[...], near_depth[...])
+    chunk(0)
+    chunk(rows - CHUNK)
+    for g in range(groups):
+        at = slice(g * group_rows, (g + 1) * group_rows)
+        merged = jnp.where(line < 4, turn(near_done, -(g * STRIP + 4)), height_out[at, :])
+        height_out[at, :] = jnp.where(
+            line >= cols - 4, turn(near_done, cols - 28 - g * STRIP), merged
+        )
 
     height_high, height_low = split(height_out[...])
     projected = dot(
@@ -487,10 +527,12 @@
             *(pltpu.VMEM(x.shape, x.dtype) for x in inputs),
             pltpu.VMEM((32, cols), F32),
             pltpu.VMEM((6, 16, cols), F32),
-            pltpu.VMEM((16, rows), F32),
-            pltpu.VMEM((16, rows), F32),
-            pltpu.VMEM((rows + 8, 2 * cols), F32),
-            pltpu.VMEM((rows + 8, 2 * cols), F32),
+            pltpu.VMEM((2, rows * STRIP // (4 * cols), cols), F32),
+            pltpu.VMEM((2, rows * STRIP // (4 * cols), cols), F32),
+            pltpu.VMEM((rows + 8, cols), F32),
+            pltpu.VMEM((rows + 8, cols), F32),
+            pltpu.VMEM((rows * STRIP // cols + 8, cols), F32),
+            pltpu.VMEM((rows * STRIP // cols + 8, cols), F32),
             packed,
             packed,
             packed,

time: 26.4 us -> 24 us (0.909)
  Pallas kernels: 24.2 us -> 21.8 us
    pallas_call x1, Pallas kernels: 24.2 us -> 21.8 us  [local(): pl.pallas_call(functools.partial(kernel, lon_count, lat_count, slot_rows)...]
where the time goes in v1:
time: 24 us; the launch traced here: 23.9 us
  Pallas kernels  21.8 us (91%)
  local copies, waits for them, and re-layouts  1.41 us (6%)
  between operations  0.64 us (3%)
    pallas_call x1, Pallas kernels, local(): pl.pallas_call(functools.partial(kernel, lon_count, lat_count, slot_rows)...  21.8 us
    unnamed x2, local copies, waits for them, and re-layouts  1.41 us

profile of v1, /device:TPU:0, one launch (start us, length us, event | category | flops | bytes accessed | tf_op | source)
XLA Modules:
  0.0 23.9 jit_solution(17629855821701851760)
XLA Ops:
  0.6 21.8 %shard_map.113 = (f32[512,128]{1,0:T(8,128)S(1)}, f32[512,128]{1,0:T(8,128)S(1)}) custom-call(f32[512,128]{1,0:T(8,128)} %height_hbm.1, f32[512,128]{1,0:T(8,128)} %depth_hbm.1, s32[512,128]{1,0:T(8,128)} %wet_hbm.1, f32[32,512]{1,0:T(8,128)} %basis_lat_hbm.1, f32[32,128]{1,0:T(8,128)} %basis_lon_hbm.1, s32[8,32]{1,0:T(8,128)} %bitcast.5, s32[8,32]{1,0:T(8,128)} %bitcast.6, ...), custom_call_target="tpu_custom_call" | custom-call | tf_op jit(solution)/shard_map/pallas_call | solution.py:518
  22.5 0.7 %copy.14 = f32[512,128]{1,0:T(8,128)} copy(f32[512,128]{1,0:T(8,128)S(1)} %get-tuple-element.2) | data formatting | bytes 524288
  23.2 0.7 %copy.15 = f32[512,128]{1,0:T(8,128)} copy(f32[512,128]{1,0:T(8,128)S(1)} %get-tuple-element.3) | data formatting | bytes 524288

commit v2 on v1

--- a/solution.py
+++ b/solution.py
@@ -141,7 +141,7 @@
             )
         )
     ]
-    for load in loads:
+    for load in loads[:3]:
         load.start()
     lat = lax.axis_index("lat")
     lon = lax.axis_index("lon")
@@ -158,7 +158,8 @@
 
     def each_peer(body):
         if lon_count <= 8:
-            for offset in range(1, lon_count):
+            half = lon_count // 2
+            for offset in sorted(range(1, lon_count), key=lambda n: abs(n - half)):
                 body(offset)
         else:
             def step(offset, carry):
@@ -176,6 +177,9 @@
     for lat_at in (up, down):
         for lon_at in (left, lon, right):
             greet(lat_at, lon_at)
+
+    for load in loads[3:]:
+        load.start()
 
     for load in loads[:3]:
         load.wait()
@@ -478,6 +482,17 @@
         copy.wait_send()
     for wait in sent:
         wait()
+
+
+def hand_over(height, gradient, height_hbm, gradient_hbm, sem):
+    copies = [
+        pltpu.make_async_copy(height, height_hbm, sem.at[0]),
+        pltpu.make_async_copy(gradient, gradient_hbm, sem.at[1]),
+    ]
+    for copy in copies:
+        copy.start()
+    for copy in copies:
+        copy.wait()
 
 
 def local(
@@ -515,7 +530,7 @@
         prior_patches.reshape(NPATCH, NPATCH),
         prior_subfaults,
     )
-    return pl.pallas_call(
+    held = pl.pallas_call(
         functools.partial(kernel, lon_count, lat_count, slot_rows),
         out_shape=(pltpu.VMEM((rows, cols), F32),) * 2,
         in_specs=[hbm] * 10,
@@ -555,6 +570,14 @@
             collective_id=0, has_side_effects=True, vmem_limit_bytes=48 * 1024 * 1024
         ),
     )(*(pltpu.with_memory_space_constraint(x, pltpu.HBM) for x in inputs))
+    vmem = pl.BlockSpec(memory_space=pltpu.VMEM)
+    return pl.pallas_call(
+        hand_over,
+        out_shape=(pltpu.HBM((rows, cols), F32),) * 2,
+        in_specs=[vmem, vmem],
+        out_specs=(hbm, hbm),
+        scratch_shapes=[pltpu.SemaphoreType.DMA((2,))],
+    )(*held)
 
 
 def solution(mesh):

time: 24 us -> 26.1 us (1.088)
  Pallas kernels: 21.8 us -> 24 us
    pallas_call x0 -> x1, Pallas kernels: none -> 1.83 us  [local(): pl.pallas_call(hand_over, out_shape=(pltpu.HBM((rows, cols), F32),) * 2,...]
    pallas_call x1, Pallas kernels: 21.8 us -> 22.1 us  [local(): pl.pallas_call(functools.partial(kernel, lon_count, lat_count, slot_rows)...]
    unnamed x2 -> x4, local copies, waits for them, and re-layouts: 1.41 us -> 1.39 us
where the time goes in v2:
time: 26.1 us; the launch traced here: 26 us
  Pallas kernels  24 us (92%)
  local copies, waits for them, and re-layouts  1.39 us (5%)
  between operations  0.65 us (2%)
    pallas_call x1, Pallas kernels, local(): pl.pallas_call(functools.partial(kernel, lon_count, lat_count, slot_rows)...  22.1 us
    pallas_call x1, Pallas kernels, local(): pl.pallas_call(hand_over, out_shape=(pltpu.HBM((rows, cols), F32),) * 2,...  1.83 us
    unnamed x4, local copies, waits for them, and re-layouts  1.39 us

profile of v2, /device:TPU:0, one launch (start us, length us, event | category | flops | bytes accessed | tf_op | source)
XLA Modules:
  0.0 26.0 jit_solution(15484965069147793470)
XLA Ops:
  0.6 22.1 %shard_map.113 = (f32[512,128]{1,0:T(8,128)S(1)}, f32[512,128]{1,0:T(8,128)S(1)}) custom-call(f32[512,128]{1,0:T(8,128)} %height_hbm.1, f32[512,128]{1,0:T(8,128)} %depth_hbm.1, s32[512,128]{1,0:T(8,128)} %wet_hbm.1, f32[32,512]{1,0:T(8,128)} %basis_lat_hbm.1, f32[32,128]{1,0:T(8,128)} %basis_lon_hbm.1, s32[8,32]{1,0:T(8,128)} %bitcast.5, s32[8,32]{1,0:T(8,128)} %bitcast.6, ...), custom_call_target="tpu_custom_call" | custom-call | tf_op jit(solution)/shard_map/pallas_call | solution.py:533
  22.8 0.0 copy-start
  22.8 0.7 %copy-done = f32[512,128]{1,0:T(8,128)} copy-done((f32[512,128]{1,0:T(8,128)}, f32[512,128]{1,0:T(8,128)S(1)}, u32[]{:S(2)}) %copy-start) | copy-done | bytes 262168
  23.4 0.0 copy-start.1
  23.4 0.7 %copy-done.1 = f32[512,128]{1,0:T(8,128)} copy-done((f32[512,128]{1,0:T(8,128)}, f32[512,128]{1,0:T(8,128)S(1)}, u32[]{:S(2)}) %copy-start.1) | copy-done | bytes 262168
  24.2 1.8 %shard_map.114 = (f32[512,128]{1,0:T(8,128)}, f32[512,128]{1,0:T(8,128)}) custom-call(f32[512,128]{1,0:T(8,128)} %copy-done, f32[512,128]{1,0:T(8,128)} %copy-done.1), custom_call_target="tpu_custom_call" | custom-call | tf_op jit(solution)/shard_map/pallas_call | solution.py:574
Async XLA Ops:
  22.8 0.7 %copy-start = (f32[512,128]{1,0:T(8,128)}, f32[512,128]{1,0:T(8,128)S(1)}, u32[]{:S(2)}) copy-start(f32[512,128]{1,0:T(8,128)S(1)} %get-tuple-element.4.height) | copy-start | bytes 786436
  23.4 0.7 %copy-start.1 = (f32[512,128]{1,0:T(8,128)}, f32[512,128]{1,0:T(8,128)S(1)}, u32[]{:S(2)}) copy-start(f32[512,128]{1,0:T(8,128)S(1)} %get-tuple-element.5.gradient) | copy-start | bytes 786436
